TPU v7x, 32 devices: a whole 2x2x4 slice. The times are simulated.
32 devices in a mesh: space: 8 (over z, y), filt: 4 (over x, core).
Axes of the slice: x: 2, y: 2, z: 4, core: 2. Of those that a mesh axis runs over, the one named last changes fastest.
Arguments:
- features: bfloat16 [128, 128, 1024], P('space', 'filt'), may hold values from -6 to 6
- grad_out: bfloat16 [128, 128, 1024], P('space', 'filt'), may hold values from -6 to 6
- weight: bfloat16 [3, 3, 128, 128], P(None, None, 'filt'), may hold values from -0.1875 to 0.1875
Outputs:
- grad_features: bfloat16 [128, 128, 1024], P('space', 'filt')
- grad_weight: float32 [3, 3, 128, 128], P(None, None, 'filt')
All inputs are finite; a program needn't handle non-finite values.
Results may differ from a plain program's by a relative error of at most 0.001.
Values may be sent and summed in bfloat16 or wider, within the bound.
A program may use at most 192 MiB of HBM per device.

v0:
```python
import jax
import jax.numpy as jnp
from jax import lax
from jax.sharding import PartitionSpec as P


def extended(array, sides, width):
    for axis, dim in sides:
        peers, length = (lax.axis_size(axis), array.shape[dim])
        up = [(i, (i + 1) % peers) for i in range(peers - 1)]
        down = [(j, i) for i, j in up]
        last = lax.slice_in_dim(array, length - width, length, axis=dim)
        initial = lax.slice_in_dim(array, 0, width, axis=dim)
        before = lax.ppermute(last, axis, up)
        after = lax.ppermute(initial, axis, down)
        array = jnp.concatenate([before, array, after], axis=dim)
    return array


def data_terms(carry, padded, taps, rows, width):
    for tap_a in range(3):
        for tap_b in range(3):
            shifted = padded[2 - tap_a : 2 - tap_a + rows, :, 2 - tap_b : 2 - tap_b + width]
            carry = carry + jnp.einsum(
                "oc,hox->hcx", taps[tap_a, tap_b], shifted, preferred_element_type=jnp.float32
            )
    return carry


def filter_taps(center, x_piece, rows, width):
    padded = jnp.pad(x_piece, ((0, 0), (0, 0), (1, 1)))
    pieces = []
    for tap_a in range(3):
        for tap_b in range(3):
            window = padded[tap_a : tap_a + rows, :, tap_b : tap_b + width]
            pieces.append(
                jnp.einsum("hox,hcx->oc", center, window, preferred_element_type=jnp.float32)
            )
    return jnp.stack(pieces).reshape(3, 3, center.shape[1], x_piece.shape[1])


def on_device(features, grad_out, weight):
    rows = features.shape[0]
    cin_local = features.shape[1]
    width = features.shape[2]
    x_ext = extended(features, (("space", 0),), 1)
    g_ext = extended(grad_out, (("space", 0),), 1)
    scale = jnp.sqrt(jnp.float32(rows * lax.axis_size("space") * width))
    taps_block = lax.all_to_all(weight, "filt", split_axis=3, concat_axis=2, tiled=True)
    g_all = lax.all_gather(g_ext, "filt", axis=1, tiled=True)
    center = g_all[1 : 1 + rows]
    local_filter = filter_taps(center, x_ext, rows, width)
    total_filter = lax.psum(local_filter, "space")
    owned_filter = lax.all_to_all(total_filter, "filt", split_axis=2, concat_axis=3, tiled=True)
    grad_weight = owned_filter / scale
    g_pad = jnp.pad(g_all, ((0, 0), (0, 0), (1, 1)))
    start_sum = jnp.zeros((rows, cin_local, width), jnp.float32)
    grad_features = data_terms(start_sum, g_pad, taps_block, rows, width).astype(jnp.bfloat16)
    return (grad_features, grad_weight)


def solution(mesh):
    in_specs = (P("space", "filt", None), P("space", "filt", None), P(None, None, "filt", None))
    out_specs = (P("space", "filt", None), P(None, None, "filt", None))
    return jax.shard_map(
        on_device, mesh=mesh, in_specs=in_specs, out_specs=out_specs, check_vma=False
    )
```

profile of v0, /device:TPU:1, one launch (start us, length us, event | category | flops | bytes accessed | tf_op | source)
XLA Modules:
  0.0 178.4 jit_solution(5676434116874900541)
XLA Ops:
  7.2 0.0 all-gather.2.cloned.1.call-start
  7.2 1.0 fusion.59
  8.2 1.3 collective-permute-start.1
  9.5 4.6 %collective-permute-start = (bf16[1,32,1024]{2,1,0:T(8,128)(2,1)S(1)}, bf16[1,32,1024]{2,1,0:T(8,128)(2,1)S(1)}, u32[]{:S(2)}, u32[]{:S(2)}) collective-permute-start(bf16[1,32,1024]{2,1,0:T(8,128)(2,1)S(1)} %get-tuple-element.4), channel_id=1, source_target_pairs={{0,4},{4,8},{8,12},{12,16},{16,20},{20,24},{24,28},{1,5},{5,9},{9,... | collective-permute-start | bytes 196616 | tf_op jit(solution)/shard_map/ppermute | solution.py:14
  14.1 2.0 %collective-permute-done = bf16[1,32,1024]{2,1,0:T(8,128)(2,1)S(1)} collective-permute-done((bf16[1,32,1024]{2,1,0:T(8,128)(2,1)S(1)}, bf16[1,32,1024]{2,1,0:T(8,128)(2,1)S(1)}, u32[]{:S(2)}, u32[]{:S(2)}) %collective-permute-start) | collective-permute-done | bytes 65568 | tf_op jit(solution)/shard_map/ppermute | solution.py:14
  16.1 2.4 %pad_maximum_fusion = bf16[18,32,1024]{2,1,0:T(8,128)(2,1)} fusion(bf16[1,32,1024]{2,1,0:T(8,128)(2,1)S(1)} %collective-permute-done.1, bf16[16,32,1024]{2,1,0:T(8,128)(2,1)} %param.4, bf16[1,32,1024]{2,1,0:T(8,128)(2,1)S(1)} %collective-permute-done), kind=kLoop, calls=%fused_computation.33 | loop fusion | flops 1179648 | bytes 2359296 | tf_op jit(solution)/shard_map/concatenate | solution.py:16
  18.5 0.0 all-gather.2.cloned.1.call-update
  18.5 0.0 all-reduce.4.cloned.1.call-start
  18.6 1.3 collective-permute-start.3
  19.9 4.9 %collective-permute-start.2 = (bf16[1,32,1024]{2,1,0:T(8,128)(2,1)S(1)}, bf16[1,32,1024]{2,1,0:T(8,128)(2,1)S(1)}, u32[]{:S(2)}, u32[]{:S(2)}) collective-permute-start(bf16[1,32,1024]{2,1,0:T(8,128)(2,1)S(1)} %get-tuple-element.2), channel_id=1, source_target_pairs={{0,4},{4,8},{8,12},{12,16},{16,20},{20,24},{24,28},{1,5},{5,9},{9,... | collective-permute-start | bytes 196616 | tf_op jit(solution)/shard_map/ppermute | solution.py:14
  24.8 0.2 copy.7
  25.1 0.3 reshape.30
  25.3 7.2 %all_to_all.27 = bf16[4,2,4608]{2,1,0:T(2,128)(2,1)S(1)} all-to-all(bf16[4,2,4608]{2,1,0:T(2,128)(2,1)S(1)} %reshape.30), channel_id=1, replica_groups=mesh['space'=8,'filt'=4] {'filt'}, dimensions={0} | all-to-all | bytes 147456 | tf_op jit(solution)/shard_map/all_to_all | solution.py:49
  32.6 0.2 reshape.31
  32.8 0.3 copy.12
  33.1 0.2 all_to_all.23
  33.3 0.7 fusion.29
  34.1 26.1 %all-gather.2.cloned.1.call-done = bf16[18,128,1024]{2,1,0:T(8,128)(2,1)} async-done(((bf16[18,32,1024]{2,1,0:T(8,128)(2,1)}), bf16[18,128,1024]{2,1,0:T(8,128)(2,1)}) %all-gather.2.cloned.1.call-update) | async-done | bytes 4718608 | tf_op jit(solution)/shard_map/all_gather | solution.py:50
  60.2 3.8 %fusion.38 = f32[9,128,32]{1,2,0:T(8,128)S(1)} fusion(bf16[18,128,1024]{2,1,0:T(8,128)(2,1)} %all-gather.2.cloned.1.call-done, bf16[18,32,1026]{2,1,0:T(8,128)(2,1)S(1)} %fusion.29), kind=kOutput, calls=%fused_computation.51 | convolution fusion | flops 134217728 | bytes 5783552 | tf_op jit(solution)/shard_map/hox,hcx->oc/dot_general | solution.py:37
  64.0 0.0 copy-done
  64.0 1.5 fusion.37
  65.6 1.6 fusion.36
  67.1 1.5 fusion.35
  68.6 1.6 fusion.34
  70.2 1.6 fusion.33
  71.8 1.5 fusion.32
  73.3 1.6 fusion.31
  74.8 1.6 fusion.30
  76.4 1.2 copy.9
  77.6 0.0 all-reduce.4.cloned.1.call-update
  77.6 3.0 %fusion = f32[16,1024,32]{1,2,0:T(8,128)S(1)} fusion(bf16[18,128,1024]{2,1,0:T(8,128)(2,1)} %all-gather.2.cloned.1.call-done, bf16[3,3,128,32]{2,3,1,0:T(8,128)(2,1)S(1)} %all_to_all.23), kind=kOutput, calls=%fused_computation | convolution fusion | flops 134217728 | bytes 6299648 | tf_op jit(solution)/shard_map/oc,hox->hcx/dot_general | solution.py:24
  80.6 5.1 %fusion.8 = f32[16,1024,32]{1,2,0:T(8,128)} fusion(bf16[18,128,1024]{2,1,0:T(8,128)(2,1)} %all-gather.2.cloned.1.call-done, bf16[3,3,128,32]{2,3,1,0:T(8,128)(2,1)S(1)} %all_to_all.23), kind=kOutput, calls=%fused_computation.8 | convolution fusion | flops 134217728 | bytes 6823936 | tf_op jit(solution)/shard_map/oc,hox->hcx/dot_general | solution.py:24
  85.7 2.8 %fusion.10 = f32[16,1024,32]{1,2,0:T(8,128)} fusion(bf16[18,128,1024]{2,1,0:T(8,128)(2,1)S(1)} %bitcast.120, bf16[3,3,128,32]{2,3,1,0:T(8,128)(2,1)S(1)} %all_to_all.23), kind=kOutput, calls=%fused_computation.10 | convolution fusion | flops 134217728 | bytes 6823936 | tf_op jit(solution)/shard_map/oc,hox->hcx/dot_general | solution.py:24
  88.5 2.0 %fusion.2 = f32[16,1024,32]{1,2,0:T(8,128)} fusion(bf16[18,128,1024]{2,1,0:T(8,128)(2,1)S(1)} %bitcast.120, bf16[3,3,128,32]{2,3,1,0:T(8,128)(2,1)S(1)} %all_to_all.23), kind=kOutput, calls=%fused_computation.2 | convolution fusion | flops 134217728 | bytes 6299648 | tf_op jit(solution)/shard_map/oc,hox->hcx/dot_general | solution.py:24
  90.5 2.8 %fusion.12 = f32[16,1024,32]{1,2,0:T(8,128)} fusion(bf16[18,128,1024]{2,1,0:T(8,128)(2,1)S(1)} %bitcast.120, bf16[3,3,128,32]{2,3,1,0:T(8,128)(2,1)S(1)} %all_to_all.23), kind=kOutput, calls=%fused_computation.12 | convolution fusion | flops 134217728 | bytes 6823936 | tf_op jit(solution)/shard_map/oc,hox->hcx/dot_general | solution.py:24
  93.3 2.7 %fusion.14 = f32[16,1024,32]{1,2,0:T(8,128)} fusion(bf16[18,128,1024]{2,1,0:T(8,128)(2,1)S(1)} %bitcast.120, bf16[3,3,128,32]{2,3,1,0:T(8,128)(2,1)S(1)} %all_to_all.23), kind=kOutput, calls=%fused_computation.14 | convolution fusion | flops 134217728 | bytes 6823936 | tf_op jit(solution)/shard_map/oc,hox->hcx/dot_general | solution.py:24
  96.0 2.0 %fusion.4 = f32[16,1024,32]{1,2,0:T(8,128)} fusion(bf16[18,128,1024]{2,1,0:T(8,128)(2,1)S(1)} %bitcast.120, bf16[3,3,128,32]{2,3,1,0:T(8,128)(2,1)S(1)} %all_to_all.23), kind=kOutput, calls=%fused_computation.4 | convolution fusion | flops 134217728 | bytes 6299648 | tf_op jit(solution)/shard_map/oc,hox->hcx/dot_general | solution.py:24
  98.0 2.7 %fusion.16 = f32[16,1024,32]{1,2,0:T(8,128)} fusion(bf16[18,128,1024]{2,1,0:T(8,128)(2,1)S(1)} %bitcast.120, bf16[3,3,128,32]{2,3,1,0:T(8,128)(2,1)S(1)} %all_to_all.23), kind=kOutput, calls=%fused_computation.16 | convolution fusion | flops 134217728 | bytes 6823936 | tf_op jit(solution)/shard_map/oc,hox->hcx/dot_general | solution.py:24
  100.7 50.7 %all-reduce.4.cloned.1.call-done = f32[3,3,128,32]{3,1,0,2:T(4,128)} async-done(((f32[3,3,128,32]{3,1,0,2:T(4,128)}), f32[3,3,128,32]{3,1,0,2:T(4,128)}) %all-reduce.4.cloned.1.call-update) | async-done | bytes 147472 | tf_op jit(solution)/shard_map/psum | solution.py:53
  151.4 2.3 %reshape.32 = f32[4,1,9216]{2,1,0:T(1,128)} reshape(f32[128,3,3,32]{3,2,1,0:T(4,128)} %bitcast.125) | data formatting | bytes 294912
  153.7 5.0 %all-to-all-start.1 = ((f32[4,1,9216]{2,1,0:T(1,128)}), f32[4,1,9216]{2,1,0:T(1,128)S(1)}, u32[]{:S(2)}, u32[]{:S(2)}) async-start(f32[4,1,9216]{2,1,0:T(1,128)} %reshape.32), calls=%async_computation.1 | async-start | bytes 294912 | tf_op jit(solution)/shard_map/all_to_all | solution.py:54
  158.7 9.3 %fusion.39 = bf16[16,32,1024]{2,1,0:T(8,128)(2,1)} fusion(f32[16,1024,32]{1,2,0:T(8,128)S(1)} %fusion, f32[16,1024,32]{1,2,0:T(8,128)} %fusion.8, f32[16,1024,32]{1,2,0:T(8,128)} %fusion.10, f32[16,1024,32]{1,2,0:T(8,128)} %fusion.2, f32[16,1024,32]{1,2,0:T(8,128)} %fusion.12, f32[16,1024,32]{1,2,0:T(8,128)} %fusion.14, f32[16,1024,32]{1,2,0:T(8,128)} %fusion.16, ...), kind=kOutput, calls=%fused_computation.52 | convolution fusion | flops 138936320 | bytes 22552576 | tf_op jit(solution)/shard_map/oc,hox->hcx/dot_general | solution.py:24
  168.0 0.5 broadcast.23
  168.5 1.0 reduce
  169.5 0.5 reshape.33
  170.0 0.2 broadcast_multiply_fusion
  170.2 0.4 copy.10
  170.6 0.9 div.16
  (15 shorter events, 0.0 us)
Async XLA Ops:
  7.2 11.4 %copy-start.1 = (bf16[16,32,1024]{2,1,0:T(8,128)(2,1)S(1)}, bf16[16,32,1024]{2,1,0:T(8,128)(2,1)}, u32[]{:S(2)}) copy-start(bf16[16,32,1024]{2,1,0:T(8,128)(2,1)} %param.3) | copy-start | bytes 3145732
  7.2 17.6 %copy-start.2 = (bf16[3,3,32,128]{3,2,1,0:T(8,128)(2,1)S(1)}, bf16[3,3,32,128]{3,2,1,0:T(8,128)(2,1)}, u32[]{:S(2)}) copy-start(bf16[3,3,32,128]{3,2,1,0:T(8,128)(2,1)} %param.5) | copy-start | bytes 221188
  7.2 53.0 %all-gather.2.cloned.1.call-start = ((), (), s32[]{:S(2)}) async-start(), calls=%async_computation.2 | async-start | bytes 5898240 | tf_op jit(solution)/shard_map/all_gather | solution.py:50
  8.2 5.9 %collective-permute-start.1 = (bf16[1,32,1024]{2,1,0:T(8,128)(2,1)S(1)}, bf16[1,32,1024]{2,1,0:T(8,128)(2,1)S(1)}, u32[]{:S(2)}, u32[]{:S(2)}) collective-permute-start(bf16[1,32,1024]{2,1,0:T(8,128)(2,1)S(1)} %get-tuple-element.5), channel_id=1, source_target_pairs={{4,0},{8,4},{12,8},{16,12},{20,16},{24,20},{28,24},{5,1},{9,5},{13... | collective-permute-start | bytes 196616 | tf_op jit(solution)/shard_map/ppermute | solution.py:15
  9.5 6.6 %collective-permute-start = (bf16[1,32,1024]{2,1,0:T(8,128)(2,1)S(1)}, bf16[1,32,1024]{2,1,0:T(8,128)(2,1)S(1)}, u32[]{:S(2)}, u32[]{:S(2)}) collective-permute-start(bf16[1,32,1024]{2,1,0:T(8,128)(2,1)S(1)} %get-tuple-element.4), channel_id=1, source_target_pairs={{0,4},{4,8},{8,12},{12,16},{16,20},{20,24},{24,28},{1,5},{5,9},{9,... | collective-permute-start | bytes 196616 | tf_op jit(solution)/shard_map/ppermute | solution.py:14
  18.5 132.9 %all-reduce.4.cloned.1.call-start = ((), (), s32[]{:S(2)}) async-start(), calls=%async_computation.3 | async-start | bytes 1572864 | tf_op jit(solution)/shard_map/psum | solution.py:53
  18.6 14.7 %collective-permute-start.3 = (bf16[1,32,1024]{2,1,0:T(8,128)(2,1)S(1)}, bf16[1,32,1024]{2,1,0:T(8,128)(2,1)S(1)}, u32[]{:S(2)}, u32[]{:S(2)}) collective-permute-start(bf16[1,32,1024]{2,1,0:T(8,128)(2,1)S(1)} %get-tuple-element.3), channel_id=1, source_target_pairs={{4,0},{8,4},{12,8},{16,12},{20,16},{24,20},{28,24},{5,1},{9,5},{13... | collective-permute-start | bytes 196616 | tf_op jit(solution)/shard_map/ppermute | solution.py:15
  19.9 13.4 %collective-permute-start.2 = (bf16[1,32,1024]{2,1,0:T(8,128)(2,1)S(1)}, bf16[1,32,1024]{2,1,0:T(8,128)(2,1)S(1)}, u32[]{:S(2)}, u32[]{:S(2)}) collective-permute-start(bf16[1,32,1024]{2,1,0:T(8,128)(2,1)S(1)} %get-tuple-element.2), channel_id=1, source_target_pairs={{0,4},{4,8},{8,12},{12,16},{16,20},{20,24},{24,28},{1,5},{5,9},{9,... | collective-permute-start | bytes 196616 | tf_op jit(solution)/shard_map/ppermute | solution.py:14
  60.2 3.9 %copy-start = (bf16[18,128,1024]{2,1,0:T(8,128)(2,1)S(1)}, bf16[18,128,1024]{2,1,0:T(8,128)(2,1)}, u32[]{:S(2)}) copy-start(bf16[18,128,1024]{2,1,0:T(8,128)(2,1)} %all-gather.2.cloned.1.call-done) | copy-start | bytes 14155780
  77.6 8.1 %slice-start = ((s8[4718592]{0:T(1024)(128)(4,1)}), s8[524288]{0:T(1024)(128)(4,1)S(1)}, s32[]{:S(2)}) async-start(s8[4718592]{0:T(1024)(128)(4,1)} %bitcast.119), calls=%async_computation.4 | async-start | bytes 1048576
  77.6 8.1 %slice-start.1 = ((s8[4718592]{0:T(1024)(128)(4,1)}), s8[4194304]{0:T(1024)(128)(4,1)S(1)}, s32[]{:S(2)}) async-start(s8[4718592]{0:T(1024)(128)(4,1)} %bitcast.119), calls=%async_computation.5 | async-start | bytes 8388608
  153.7 14.3 %all-to-all-start.1 = ((f32[4,1,9216]{2,1,0:T(1,128)}), f32[4,1,9216]{2,1,0:T(1,128)S(1)}, u32[]{:S(2)}, u32[]{:S(2)}) async-start(f32[4,1,9216]{2,1,0:T(1,128)} %reshape.32), calls=%async_computation.1 | async-start | bytes 294912 | tf_op jit(solution)/shard_map/all_to_all | solution.py:54
Sparse Core Ops, SparseCore 0:
  18.7 41.4 all-gather.1
  77.7 73.6 all-reduce.3
where the time goes:
time: 179 us; the launch traced here: 178 us
  waiting for transfers between devices  78.9 us (44%)
  matrix products  48.5 us (27%)
  starting transfers between devices  17.1 us (10%)
  between operations  14.2 us (8%)
  local copies, waits for them, and re-layouts  8.02 us (4%)
  blocking collectives  7.25 us (4%)
  other arithmetic  4.37 us (2%)
    psum x1, waiting for transfers between devices, on_device(): total_filter = lax.psum(local_filter, 'space')  50.7 us
    dot_general x9, matrix products, data_terms(): jnp.einsum('oc,hox->hcx', taps[tap_a, tap_b], shifted, preferred_element_...  32.3 us
    all_gather x1, waiting for transfers between devices, on_device(): g_all = lax.all_gather(g_ext, 'filt', axis=1, tiled=True)  26.1 us
    dot_general x9, matrix products, filter_taps(): jnp.einsum('hox,hcx->oc', center, window, preferred_element_type=jnp.floa...  16.2 us
    ppermute x2, starting transfers between devices, extended(): before = lax.ppermute(last, axis, up)  9.48 us
    all_to_all x1, blocking collectives, on_device(): lax.all_to_all(weight, 'filt', split_axis=3, concat_axis=2, tiled=True)  7.25 us
    all_to_all x1, starting transfers between devices, on_device(): lax.all_to_all(total_filter, 'filt', split_axis=2, concat_axis=3, tiled=T...  4.98 us
  transfers between devices with their start and end apart: 7, of which 3 were waited for; matrix products, arithmetic and copies ran while one was open for 19% of the time, Pallas kernels for 0%

commit v1 on v0

v1 whole, which is shorter than its diff:
```python
import functools

import jax
import jax.numpy as jnp
from jax import lax
from jax.experimental import pallas as pl
from jax.experimental.pallas import tpu as pltpu
from jax.sharding import PartitionSpec as P

MESH = pl.DeviceIdType.MESH
NT = (((1,), (1,)), ((), ()))
PIECES = 8


def kernel(n, rows, ch, width, x_ref, g_ref, w_ref, out_ref, gw_ref,
           gall, xraw, xs, wall, wlhs, fs, rs, red,
           loc, sib_s, sib_r, px_s, px_r, fw_s, fw_r, hg_s, hg_r, hx_s, hx_r,
           w_s, w_r, rs_s, rs_r, ag_s, ag_r):
    s = lax.axis_index("space")
    f = lax.axis_index("filt")
    total = 4 * n
    me = s * 4 + f
    sib = f + 1 - 2 * lax.rem(f, 2)
    far = lax.rem(f + 2, 4)
    diag = lax.rem(sib + 2, 4)
    peers = (f, sib, far, diag)
    stride = n // PIECES
    steps = (rows - 2) // 2

    barrier = pltpu.get_barrier_semaphore()

    def greet(i, carry):
        t = lax.rem(me + i, total)
        pl.semaphore_signal(barrier, inc=1, device_id=(t // 4, lax.rem(t, 4)), device_id_type=MESH)
        return carry

    lax.fori_loop(1, total, greet, 0)

    local_g = pltpu.make_async_copy(g_ref, gall.at[pl.ds(1, rows), pl.ds(0, ch)], loc.at[0])
    local_x = pltpu.make_async_copy(x_ref, xraw.at[pl.ds(1, rows)], loc.at[1])
    local_w = pltpu.make_async_copy(w_ref.at[f], wall.at[pl.ds(0, ch)], loc.at[2])
    local_g.start()
    local_x.start()
    local_w.start()
    pl.semaphore_wait(barrier, total - 1)

    def remote(src, dst, ssem, rsem, dev):
        return pltpu.make_async_remote_copy(
            src_ref=src, dst_ref=dst, send_sem=ssem, recv_sem=rsem,
            device_id=dev, device_id_type=MESH)

    def across(first, count, c):
        return remote(g_ref.at[pl.ds(first, count)],
                      gall.at[pl.ds(first + 1, count), pl.ds(2 * ch, ch)],
                      px_s.at[c], px_r.at[c], (s, far))

    def forward(first, count, c):
        return remote(gall.at[pl.ds(first + 1, count), pl.ds(2 * ch, ch)],
                      gall.at[pl.ds(first + 1, count), pl.ds(3 * ch, ch)],
                      fw_s.at[c], fw_r.at[c], (s, sib))

    def edge_rows(k):
        return (0 if k == 0 else rows - 1, 1, k)

    def weights(p):
        return remote(w_ref.at[peers[p]], wall.at[pl.ds(p * ch, ch)], w_s.at[p], w_r.at[p],
                      (s, peers[p]))

    to_sib = remote(g_ref, gall.at[pl.ds(1, rows), pl.ds(ch, ch)], sib_s, sib_r, (s, sib))

    def halo_g(p, d):
        part = pl.ds(p * ch, ch)
        src = gall.at[rows if d == 0 else 1, part] if p else g_ref.at[rows - 1 if d == 0 else 0]
        return remote(src, gall.at[0 if d == 0 else rows + 1, part],
                      hg_s.at[p, d], hg_r.at[p, d], (s + 1 if d == 0 else s - 1, f))

    def halo_x(d):
        return remote(x_ref.at[rows - 1 if d == 0 else 0], xraw.at[0 if d == 0 else rows + 1],
                      hx_s.at[d], hx_r.at[d], (s + 1 if d == 0 else s - 1, f))

    has_next = s < n - 1
    has_prev = s > 0

    def send_halo(p):
        @pl.when(has_next)
        def _():
            halo_g(p, 0).start()

        @pl.when(has_prev)
        def _():
            halo_g(p, 1).start()

    across(*edge_rows(0)).start()
    across(*edge_rows(1)).start()
    for p in (2, 3, 1):
        weights(p).start()

    def start_across(k, carry):
        across(1 + 2 * k, 2, 2 + k).start()
        return carry

    lax.fori_loop(0, steps, start_across, 0)
    to_sib.start()

    @pl.when(has_next)
    def _():
        halo_x(0).start()

    @pl.when(has_prev)
    def _():
        halo_x(1).start()

    send_halo(0)

    @pl.when(jnp.logical_not(has_prev))
    def _():
        gall[0] = jnp.zeros(gall.shape[1:], gall.dtype)
        xraw[0] = jnp.zeros(xraw.shape[1:], xraw.dtype)

    @pl.when(jnp.logical_not(has_next))
    def _():
        gall[rows + 1] = jnp.zeros(gall.shape[1:], gall.dtype)
        xraw[rows + 1] = jnp.zeros(xraw.shape[1:], xraw.dtype)

    lane = lax.broadcasted_iota(jnp.int32, (ch, width), 1)

    def from_left(v):
        return jnp.where(lane == 0, 0.0, pltpu.roll(v, 1, 1))

    def from_right(v):
        return jnp.where(lane == width - 1, 0.0, pltpu.roll(v, width - 1, 1))

    def shift_x(r, carry):
        v = xraw[r]
        vf = v.astype(jnp.float32)
        xs[r, pl.ds(0, ch), :] = from_left(vf).astype(jnp.bfloat16)
        xs[r, pl.ds(ch, ch), :] = v
        xs[r, pl.ds(2 * ch, ch), :] = from_right(vf).astype(jnp.bfloat16)
        return carry

    local_x.wait()
    lax.fori_loop(1, rows + 1, shift_x, 0)

    for k in range(2):
        across(*edge_rows(k)).wait_recv()
        forward(*edge_rows(k)).start()
    send_halo(2)
    local_g.wait()
    to_sib.wait_recv()
    send_halo(1)
    for k in range(2):
        forward(*edge_rows(k)).wait_recv()
    send_halo(3)

    local_w.wait()
    for p in range(1, 4):
        weights(p).wait_recv()
    for r in range(3):
        block = wall[:, r * 128:(r + 1) * 128].astype(jnp.float32)
        wlhs[:, r * 128:(r + 1) * 128] = block.T[:3 * ch].astype(jnp.bfloat16)

    @pl.when(has_prev)
    def _():
        halo_x(0).wait_recv()

    @pl.when(has_next)
    def _():
        halo_x(1).wait_recv()

    shift_x(0, 0)
    shift_x(rows + 1, 0)

    def filter_row(h, part, acc):
        g = gall[h + 1, part * 2 * ch:(part + 1) * 2 * ch, :]
        v = xs[pl.ds(h, 3)].reshape(9 * ch, width)
        return acc + lax.dot_general(g, v, NT, preferred_element_type=jnp.float32)

    def data_row(h):
        g = gall[pl.ds(h, 3)].reshape(12 * ch, width)
        r = jnp.dot(wlhs[...], g, preferred_element_type=jnp.float32)
        out = r[ch:2 * ch] + from_right(r[:ch]) + from_left(r[2 * ch:])
        out_ref[h] = out.astype(out_ref.dtype)

    q = s // stride
    owner = lax.rem(s, stride) == 0

    def piece_out(part, dest):
        return remote(fs.at[part, dest], rs.at[part, s], rs_s.at[part, dest], rs_r.at[part, s],
                      (dest * stride, f))

    def piece_in(part, src):
        return remote(fs.at[part, 0], rs.at[part, src], rs_s.at[part, 0], rs_r.at[part, src], (s, f))

    def scatter(part, acc):
        fs[part] = acc.reshape(PIECES, 8, 9 * ch)

        def send(i, carry):
            dest = lax.rem(q + i, PIECES)

            @pl.when(dest * stride != s)
            def _():
                piece_out(part, dest).start()

            return carry

        lax.fori_loop(0, PIECES, send, 0)

    def final_out(part, t):
        low = q < PIECES // 2
        home = jnp.where(low, peers[2 * part], peers[2 * part + 1])
        slot = lax.rem(q, PIECES // 2)
        return home, remote(red.at[part], gw_ref.at[f, slot], ag_s.at[part, t],
                            ag_r.at[part, q], (t, home))

    def final_in(part, k):
        src = peers[2 * part + k // (PIECES // 2)]
        slot = k % (PIECES // 2)
        return remote(red.at[part], gw_ref.at[src, slot], ag_s.at[part, 0], ag_r.at[part, k], (s, f))

    def reduce(part):
        @pl.when(owner)
        def _():
            def add(i, acc):
                src = lax.rem(s + i, n)
                piece_in(part, src).wait_recv()
                return acc + rs[part, src]

            red[part] = lax.fori_loop(1, n, add, fs[part, q])

            def send(i, carry):
                t = lax.rem(s + i, n)
                home, copy = final_out(part, t)

                @pl.when(jnp.logical_or(t != s, home != f))
                def _():
                    copy.start()

                return carry

            lax.fori_loop(0, n, send, 0)
            if part == 0:
                @pl.when(q < PIECES // 2)
                def _():
                    gw_ref[f, lax.rem(q, PIECES // 2)] = red[part]

    def finish(part):
        for k in range(PIECES):
            if part == 0 and k < PIECES // 2:
                @pl.when(s != k * stride)
                def _():
                    final_in(part, k).wait_recv()
            else:
                final_in(part, k).wait_recv()

        def sent(i, carry):
            dest = lax.rem(q + i, PIECES)

            @pl.when(dest * stride != s)
            def _():
                piece_out(part, dest).wait_send()

            return carry

        lax.fori_loop(0, PIECES, sent, 0)

        @pl.when(owner)
        def _():
            def sent_final(i, carry):
                t = lax.rem(s + i, n)
                home, copy = final_out(part, t)

                @pl.when(jnp.logical_or(t != s, home != f))
                def _():
                    copy.wait_send()

                return carry

            lax.fori_loop(0, n, sent_final, 0)

    zero = jnp.zeros((2 * ch, 9 * ch), jnp.float32)
    acc = lax.fori_loop(0, rows, lambda h, a: filter_row(h, 0, a), zero)
    scatter(0, acc)

    for p in range(4):
        @pl.when(has_prev)
        def _():
            halo_g(p, 0).wait_recv()

        @pl.when(has_next)
        def _():
            halo_g(p, 1).wait_recv()

    acc = filter_row(0, 1, zero)
    acc = filter_row(rows - 1, 1, acc)

    def arrive(k):
        across(1 + 2 * k, 2, 2 + k).wait_recv()
        forward(1 + 2 * k, 2, 2 + k).start()
        forward(1 + 2 * k, 2, 2 + k).wait_recv()

    def step(k, acc):
        arrive(k)
        acc = filter_row(1 + 2 * k, 1, acc)
        acc = filter_row(2 + 2 * k, 1, acc)
        data_row(2 * k)
        data_row(2 * k + 1)
        return acc

    middle = steps // 2
    acc = lax.fori_loop(0, middle, step, acc)
    reduce(0)
    acc = lax.fori_loop(middle, steps - 1, step, acc)
    arrive(steps - 1)
    acc = filter_row(rows - 3, 1, acc)
    acc = filter_row(rows - 2, 1, acc)
    scatter(1, acc)

    def last(h, carry):
        data_row(h)
        return carry

    lax.fori_loop(rows - 4, rows, last, 0)
    reduce(1)

    for k in range(2):
        across(*edge_rows(k)).wait_send()
        forward(*edge_rows(k)).wait_send()

    def sent_rows(k, carry):
        across(1 + 2 * k, 2, 2 + k).wait_send()
        forward(1 + 2 * k, 2, 2 + k).wait_send()
        return carry

    lax.fori_loop(0, steps, sent_rows, 0)
    to_sib.wait_send()
    for p in range(1, 4):
        weights(p).wait_send()

    @pl.when(has_next)
    def _():
        halo_x(0).wait_send()
        for p in range(4):
            halo_g(p, 0).wait_send()

    @pl.when(has_prev)
    def _():
        halo_x(1).wait_send()
        for p in range(4):
            halo_g(p, 1).wait_send()

    finish(0)
    finish(1)


def on_device(features, grad_out, weight):
    n = lax.axis_size("space")
    rows, ch, width = features.shape
    scale = jnp.sqrt(jnp.float32(rows * n * width))
    w = weight[::-1].reshape(3, 3, ch, 4, ch).transpose(3, 2, 0, 1, 4).reshape(4, ch, 3, 3 * ch)
    w = jnp.pad(w, ((0, 0), (0, 0), (0, 0), (0, 128 - 3 * ch))).reshape(4, ch, 384)
    chunks = 2 + (rows - 2) // 2
    dma = pltpu.SemaphoreType.DMA
    half = PIECES // 2
    flops = 4 * 9 * 4 * ch * ch * rows * width
    grad_features, raw = pl.pallas_call(
        functools.partial(kernel, n, rows, ch, width),
        out_shape=(jax.ShapeDtypeStruct((rows, ch, width), jnp.bfloat16),
                   jax.ShapeDtypeStruct((4, half, 8, 9 * ch), jnp.float32)),
        in_specs=[pl.BlockSpec(memory_space=pl.ANY)] * 3,
        out_specs=(pl.BlockSpec(memory_space=pltpu.VMEM), pl.BlockSpec(memory_space=pltpu.VMEM)),
        scratch_shapes=[
            pltpu.VMEM((rows + 2, 4 * ch, width), jnp.bfloat16),
            pltpu.VMEM((rows + 2, ch, width), jnp.bfloat16),
            pltpu.VMEM((rows + 2, 3 * ch, width), jnp.bfloat16),
            pltpu.VMEM((4 * ch, 384), jnp.bfloat16),
            pltpu.VMEM((3 * ch, 384), jnp.bfloat16),
            pltpu.VMEM((2, PIECES, 8, 9 * ch), jnp.float32),
            pltpu.VMEM((2, n, 8, 9 * ch), jnp.float32),
            pltpu.VMEM((2, 8, 9 * ch), jnp.float32),
            dma((3,)), dma, dma, dma((chunks,)), dma((chunks,)), dma((chunks,)), dma((chunks,)),
            dma((4, 2)), dma((4, 2)), dma((2,)), dma((2,)), dma((4,)), dma((4,)),
            dma((2, PIECES)), dma((2, n)), dma((2, n)), dma((2, PIECES)),
        ],
        compiler_params=pltpu.CompilerParams(
            collective_id=0, has_side_effects=True, vmem_limit_bytes=40 * 1024 * 1024),
        cost_estimate=pl.CostEstimate(flops=flops, bytes_accessed=8 * 1024 * 1024, transcendentals=0),
    )(features, grad_out, w)
    raw = raw.reshape(4, ch, 3, 3, ch).transpose(2, 3, 1, 0, 4).reshape(3, 3, ch, 4 * ch)
    return (grad_features, raw / scale)


def solution(mesh):
    in_specs = (P("space", "filt", None), P("space", "filt", None), P(None, None, "filt", None))
    out_specs = (P("space", "filt", None), P(None, None, "filt", None))
    return jax.shard_map(
        on_device, mesh=mesh, in_specs=in_specs, out_specs=out_specs, check_vma=False
    )
```

time: 179 us -> 53 us (0.30)
  waiting for transfers between devices: 78.9 us -> 0 us
  matrix products: 48.5 us -> 0 us
  Pallas kernels: 0 us -> 47.1 us
  starting transfers between devices: 17.1 us -> 0 us
  between operations: 14.2 us -> 0.71 us
  blocking collectives: 7.25 us -> 0 us
  other arithmetic: 4.37 us -> 0.02 us
  local copies, waits for them, and re-layouts: 8.02 us -> 4.99 us
    psum x1 -> x0, waiting for transfers between devices: 50.7 us -> none  [on_device(): total_filter = lax.psum(local_filter, 'space')]
    dot_general x18 -> x0, matrix products: 48.5 us -> none  [the longest x9 32.3 us: data_terms(): jnp.einsum('oc,hox->hcx', taps[tap_a, tap_b], shifted, preferred_element_...]
    pallas_call x0 -> x1, Pallas kernels: none -> 47.1 us  [on_device(): pl.pallas_call(functools.partial(kernel, n, rows, ch, width), out_shape=(...]
    all_gather x1 -> x0, waiting for transfers between devices: 26.1 us -> none  [on_device(): g_all = lax.all_gather(g_ext, 'filt', axis=1, tiled=True)]
    ppermute x4 -> x0, starting transfers between devices: 12.1 us -> none  [the longest x2 9.48 us: extended(): before = lax.ppermute(last, axis, up)]
    all_to_all x1 -> x0, blocking collectives: 7.25 us -> none  [on_device(): lax.all_to_all(weight, 'filt', split_axis=3, concat_axis=2, tiled=True)]
    all_to_all x1 -> x0, starting transfers between devices: 4.98 us -> none  [on_device(): lax.all_to_all(total_filter, 'filt', split_axis=2, concat_axis=3, tiled=T...]
    concatenate x2 -> x0, other arithmetic: 3.13 us -> none  [extended(): array = jnp.concatenate([before, array, after], axis=dim)]
  transfers between devices with their start and end apart: 7 -> 0, of which waited for: 3 -> 0; matrix products, arithmetic and copies ran while one was open for 19% -> 0% of each run, Pallas kernels for 0% -> 0%
where the time goes in v1:
time: 53 us; the launch traced here: 52.8 us
  Pallas kernels  47.1 us (89%)
  local copies, waits for them, and re-layouts  4.99 us (9%)
  between operations  0.71 us (1%)
    pallas_call x1, Pallas kernels, on_device(): pl.pallas_call(functools.partial(kernel, n, rows, ch, width), out_shape=(...  47.1 us
    unnamed x6, local copies, waits for them, and re-layouts  1.69 us
    div x3, local copies, waits for them, and re-layouts, on_device(): return (grad_features, raw / scale)  1.64 us

profile of v1, /device:TPU:1, one launch (start us, length us, event | category | flops | bytes accessed | tf_op | source)
XLA Modules:
  0.0 52.8 jit_solution(14296372698643028121)
XLA Ops:
  0.6 0.9 %rev.3 = bf16[3,3,32,128]{3,2,1,0:T(8,128)(2,1)S(1)} reverse(bf16[3,3,32,128]{3,2,1,0:T(8,128)(2,1)} %param.5), dimensions={0} | reverse | bytes 147456 | tf_op jit(solution)/shard_map/rev | solution.py:359
  1.5 0.0 copy-start
  1.5 0.0 copy-start.1
  1.5 0.2 reshape.19
  1.7 0.3 copy.14
  2.0 0.2 reshape.20
  2.2 0.1 copy.12
  2.2 0.1 pad.4.clone
  2.3 0.1 reshape.21.w_ref
  2.4 0.3 copy-done
  2.7 0.3 copy-done.1
  3.1 47.1 %shard_map.50 = (bf16[16,32,1024]{2,1,0:T(8,128)(2,1)S(1)}, f32[4,4,8,288]{3,2,1,0:T(8,128)S(1)}) custom-call(bf16[16,32,1024]{2,1,0:T(8,128)(2,1)S(1)} %copy-done, bf16[16,32,1024]{2,1,0:T(8,128)(2,1)S(1)} %copy-done.1, bf16[4,32,384]{2,1,0:T(8,128)(2,1)S(1)} %reshape.21.w_ref), custom_call_target="tpu_custom_call" | custom-call | flops 2415919104 | bytes 8388608 | tf_op jit(solution)/shard_map/pallas_call | solution.py:365
  50.2 0.3 div.14
  50.5 0.4 copy.11
  50.9 0.9 %div.16 = f32[3,3,32,128]{3,2,1,0:T(8,128)} reshape(f32[3,3,32,4,32]{4,3,2,1,0:T(4,128)S(1)} %copy.11) | data formatting | bytes 294912 | tf_op jit(solution)/shard_map/div | solution.py:389
  51.9 1.0 %copy.16 = bf16[16,32,1024]{2,1,0:T(8,128)(2,1)} copy(bf16[16,32,1024]{2,1,0:T(8,128)(2,1)S(1)} %get-tuple-element.8) | data formatting | bytes 2097152
  (1 shorter events, 0.0 us)
Async XLA Ops:
  1.5 1.2 %copy-start = (bf16[16,32,1024]{2,1,0:T(8,128)(2,1)S(1)}, bf16[16,32,1024]{2,1,0:T(8,128)(2,1)}, u32[]{:S(2)}) copy-start(bf16[16,32,1024]{2,1,0:T(8,128)(2,1)} %x_ref.1) | copy-start | bytes 3145732
  1.5 1.5 %copy-start.1 = (bf16[16,32,1024]{2,1,0:T(8,128)(2,1)S(1)}, bf16[16,32,1024]{2,1,0:T(8,128)(2,1)}, u32[]{:S(2)}) copy-start(bf16[16,32,1024]{2,1,0:T(8,128)(2,1)} %g_ref.1) | copy-start | bytes 3145732

commit v2 on v1

--- a/solution.py
+++ b/solution.py
@@ -81,6 +81,22 @@
     has_next = s < n - 1
     has_prev = s > 0
 
+    def share_halo(p, d):
+        row = 0 if d == 0 else rows + 1
+        return remote(gall.at[row, pl.ds(p * ch, ch)], gall.at[row, pl.ds((p + 1) * ch, ch)],
+                      hg_s.at[p + 1, d], hg_r.at[p + 1, d], (s, sib))
+
+    def pass_halo(p):
+        @pl.when(has_prev)
+        def _():
+            halo_g(p, 0).wait_recv()
+            share_halo(p, 0).start()
+
+        @pl.when(has_next)
+        def _():
+            halo_g(p, 1).wait_recv()
+            share_halo(p, 1).start()
+
     def send_halo(p):
         @pl.when(has_next)
         def _():
@@ -147,16 +163,11 @@
     send_halo(2)
     local_g.wait()
     to_sib.wait_recv()
-    send_halo(1)
-    for k in range(2):
-        forward(*edge_rows(k)).wait_recv()
-    send_halo(3)
-
     local_w.wait()
     for p in range(1, 4):
         weights(p).wait_recv()
     for r in range(3):
-        block = wall[:, r * 128:(r + 1) * 128].astype(jnp.float32)
+        block = wall[:, (2 - r) * 128:(3 - r) * 128].astype(jnp.float32)
         wlhs[:, r * 128:(r + 1) * 128] = block.T[:3 * ch].astype(jnp.bfloat16)
 
     @pl.when(has_prev)
@@ -280,37 +291,40 @@
     zero = jnp.zeros((2 * ch, 9 * ch), jnp.float32)
     acc = lax.fori_loop(0, rows, lambda h, a: filter_row(h, 0, a), zero)
     scatter(0, acc)
-
-    for p in range(4):
-        @pl.when(has_prev)
-        def _():
-            halo_g(p, 0).wait_recv()
-
-        @pl.when(has_next)
-        def _():
-            halo_g(p, 1).wait_recv()
-
-    acc = filter_row(0, 1, zero)
-    acc = filter_row(rows - 1, 1, acc)
+    pass_halo(0)
 
     def arrive(k):
         across(1 + 2 * k, 2, 2 + k).wait_recv()
         forward(1 + 2 * k, 2, 2 + k).start()
+
+    def arrive_far(k):
         forward(1 + 2 * k, 2, 2 + k).wait_recv()
+
+    for k in range(2):
+        forward(*edge_rows(k)).wait_recv()
+    acc = filter_row(0, 1, zero)
+    acc = filter_row(rows - 1, 1, acc)
 
     def step(k, acc):
         arrive(k)
-        acc = filter_row(1 + 2 * k, 1, acc)
-        acc = filter_row(2 + 2 * k, 1, acc)
-        data_row(2 * k)
-        data_row(2 * k + 1)
+        arrive_far(k - 1)
+        acc = filter_row(2 * k - 1, 1, acc)
+        acc = filter_row(2 * k, 1, acc)
+
+        @pl.when(k > 1)
+        def _():
+            data_row(2 * k - 2)
+
+        data_row(2 * k - 1)
         return acc
 
-    middle = steps // 2
-    acc = lax.fori_loop(0, middle, step, acc)
+    middle = (steps + 1) // 2
+    arrive(0)
+    acc = lax.fori_loop(1, middle, step, acc)
+    pass_halo(2)
     reduce(0)
-    acc = lax.fori_loop(middle, steps - 1, step, acc)
-    arrive(steps - 1)
+    acc = lax.fori_loop(middle, steps, step, acc)
+    arrive_far(steps - 1)
     acc = filter_row(rows - 3, 1, acc)
     acc = filter_row(rows - 2, 1, acc)
     scatter(1, acc)
@@ -319,7 +333,18 @@
         data_row(h)
         return carry
 
-    lax.fori_loop(rows - 4, rows, last, 0)
+    lax.fori_loop(rows - 4, rows - 1, last, 0)
+    for p in (0, 2):
+        @pl.when(has_prev)
+        def _():
+            share_halo(p, 0).wait_recv()
+
+        @pl.when(has_next)
+        def _():
+            share_halo(p, 1).wait_recv()
+
+    data_row(0)
+    data_row(rows - 1)
     reduce(1)
 
     for k in range(2):
@@ -339,14 +364,16 @@
     @pl.when(has_next)
     def _():
         halo_x(0).wait_send()
-        for p in range(4):
+        for p in (0, 2):
             halo_g(p, 0).wait_send()
+            share_halo(p, 1).wait_send()
 
     @pl.when(has_prev)
     def _():
         halo_x(1).wait_send()
-        for p in range(4):
+        for p in (0, 2):
             halo_g(p, 1).wait_send()
+            share_halo(p, 0).wait_send()
 
     finish(0)
     finish(1)
@@ -356,7 +383,7 @@
     n = lax.axis_size("space")
     rows, ch, width = features.shape
     scale = jnp.sqrt(jnp.float32(rows * n * width))
-    w = weight[::-1].reshape(3, 3, ch, 4, ch).transpose(3, 2, 0, 1, 4).reshape(4, ch, 3, 3 * ch)
+    w = weight.reshape(3, 3, ch, 4, ch).transpose(3, 2, 0, 1, 4).reshape(4, ch, 3, 3 * ch)
     w = jnp.pad(w, ((0, 0), (0, 0), (0, 0), (0, 128 - 3 * ch))).reshape(4, ch, 384)
     chunks = 2 + (rows - 2) // 2
     dma = pltpu.SemaphoreType.DMA

time: 53 us -> 49.7 us (0.938)
  Pallas kernels: 47.1 us -> 44.4 us
    pallas_call x1, Pallas kernels: 47.1 us -> 44.4 us  [on_device(): pl.pallas_call(functools.partial(kernel, n, rows, ch, width), out_shape=(...]
    reshape x3, local copies, waits for them, and re-layouts: 0.61 us -> 1.64 us  [on_device(): weight.reshape(3, 3, ch, 4, ch).transpose(3, 2, 0, 1, 4)]
    rev x1 -> x0, local copies, waits for them, and re-layouts: 0.89 us -> none  [on_device(): weight[::-1].reshape(3, 3, ch, 4, ch).transpose(3, 2, 0, 1, 4)]
    unnamed x6, local copies, waits for them, and re-layouts: 1.69 us -> 1.05 us
where the time goes in v2:
time: 49.7 us; the launch traced here: 49.6 us
  Pallas kernels  44.4 us (89%)
  local copies, waits for them, and re-layouts  4.48 us (9%)
  between operations  0.74 us (1%)
    pallas_call x1, Pallas kernels, on_device(): pl.pallas_call(functools.partial(kernel, n, rows, ch, width), out_shape=(...  44.4 us
    reshape x3, local copies, waits for them, and re-layouts, on_device(): weight.reshape(3, 3, ch, 4, ch).transpose(3, 2, 0, 1, 4)  1.64 us
    div x3, local copies, waits for them, and re-layouts, on_device(): return (grad_features, raw / scale)  1.64 us
    unnamed x6, local copies, waits for them, and re-layouts  1.05 us

profile of v2, /device:TPU:1, one launch (start us, length us, event | category | flops | bytes accessed | tf_op | source)
XLA Modules:
  0.0 49.6 jit_solution(8876177184098746657)
XLA Ops:
  0.6 0.0 copy-start.1
  0.6 0.0 copy-start
  0.6 1.2 %reshape.19 = bf16[3,3,32,4,32]{4,3,2,1,0:T(4,128)(2,1)S(1)} reshape(bf16[3,3,32,128]{3,2,1,0:T(8,128)(2,1)} %param.5) | data formatting | bytes 147456 | tf_op jit(solution)/shard_map/reshape | solution.py:386
  1.8 0.3 copy.14
  2.1 0.2 reshape.20
  2.3 0.1 copy.12
  2.4 0.1 pad.4.clone
  2.5 0.1 reshape.21.w_ref
  2.6 0.0 copy-done.1
  2.6 0.0 copy-done
  2.6 44.4 %shard_map.50 = (bf16[16,32,1024]{2,1,0:T(8,128)(2,1)S(1)}, f32[4,4,8,288]{3,2,1,0:T(8,128)S(1)}) custom-call(bf16[16,32,1024]{2,1,0:T(8,128)(2,1)S(1)} %copy-done, bf16[16,32,1024]{2,1,0:T(8,128)(2,1)S(1)} %copy-done.1, bf16[4,32,384]{2,1,0:T(8,128)(2,1)S(1)} %reshape.21.w_ref), custom_call_target="tpu_custom_call" | custom-call | flops 2415919104 | bytes 8388608 | tf_op jit(solution)/shard_map/pallas_call | solution.py:392
  47.0 0.3 div.14
  47.3 0.4 copy.11
  47.7 0.9 %div.16 = f32[3,3,32,128]{3,2,1,0:T(8,128)} reshape(f32[3,3,32,4,32]{4,3,2,1,0:T(4,128)S(1)} %copy.11) | data formatting | bytes 294912 | tf_op jit(solution)/shard_map/div | solution.py:416
  48.6 1.0 %copy.16 = bf16[16,32,1024]{2,1,0:T(8,128)(2,1)} copy(bf16[16,32,1024]{2,1,0:T(8,128)(2,1)S(1)} %get-tuple-element.8) | data formatting | bytes 2097152
  (1 shorter events, 0.0 us)
Async XLA Ops:
  0.6 1.9 %copy-start.1 = (bf16[16,32,1024]{2,1,0:T(8,128)(2,1)S(1)}, bf16[16,32,1024]{2,1,0:T(8,128)(2,1)}, u32[]{:S(2)}) copy-start(bf16[16,32,1024]{2,1,0:T(8,128)(2,1)} %g_ref.1) | copy-start | bytes 3145732
  0.6 1.9 %copy-start = (bf16[16,32,1024]{2,1,0:T(8,128)(2,1)S(1)}, bf16[16,32,1024]{2,1,0:T(8,128)(2,1)}, u32[]{:S(2)}) copy-start(bf16[16,32,1024]{2,1,0:T(8,128)(2,1)} %x_ref.1) | copy-start | bytes 3145732
